TPU v7x, 256 devices: a whole 4x4x8 slice. The times are simulated.
256 devices in a mesh: seq: 64 (over y, z_lo, x), fsdp: 4 (over z_hi, core).
Axes of the slice: x: 4, y: 4, z: 8 (z_hi: 2, z_lo: 4; z = z_hi * 4 + z_lo), core: 2. Of those that a mesh axis runs over, the one named last changes fastest.
Arguments:
- queries: bfloat16 [4, 128, 256, 1152], P('fsdp', 'seq'), may hold values from -36 to 36
- keys: bfloat16 [4, 128, 256, 1152], P('fsdp', 'seq'), may hold values from -5 to 5
- values: bfloat16 [4, 128, 256, 1152], P('fsdp', 'seq'), may hold values from -6 to 6
- cotangent: bfloat16 [4, 128, 256, 1152], P('fsdp', 'seq'), may hold values from -16 to 16
- out_weight: bfloat16 [1152, 1152], P('fsdp'), may hold values from -0.1875 to 0.1875
Outputs:
- output: bfloat16 [4, 128, 256, 1152], P('fsdp', 'seq')
- query_grad: bfloat16 [4, 128, 256, 1152], P('fsdp', 'seq')
- key_grad: bfloat16 [4, 128, 256, 1152], P('fsdp', 'seq')
- value_grad: bfloat16 [4, 128, 256, 1152], P('fsdp', 'seq')
- weight_grad: float32 [1152, 1152], P('fsdp', 'seq')
All inputs are finite; a program needn't handle non-finite values.
Results may differ from a plain program's by a relative error of at most 0.0058.
Values may be sent and summed in bfloat16 or wider, within the bound.
No kernel may reach another device: no remote copies, remote signals or barrier semaphores. Data moves between devices by JAX's collectives and lax.ppermute only.
A program may use at most 128 MiB of HBM per device.

v0:
```python
import jax
import jax.numpy as jnp
from jax import lax
from jax.sharding import PartitionSpec as P

HEADS = 16
HEAD_DIM = 72


def heads_view(tensor):
    return tensor.reshape(tensor.shape[0], tensor.shape[1], HEADS, HEAD_DIM)


def attend(query_rows, key_rows, value_rows):
    factor = HEAD_DIM ** (-0.5)
    scores = (
        jnp.einsum(
            "fphd,ephd->phfe",
            heads_view(query_rows),
            heads_view(key_rows),
            preferred_element_type=jnp.float32,
        )
        * factor
    )
    row_max = jnp.max(scores, axis=-1, keepdims=True)
    raised = jnp.exp(scores - row_max)
    probability = raised / jnp.sum(raised, axis=-1, keepdims=True)
    prob_low = probability.astype(jnp.bfloat16)
    attended = jnp.einsum(
        "phfe,ephd->fphd", prob_low, heads_view(value_rows), preferred_element_type=jnp.float32
    ).astype(jnp.bfloat16)
    return (attended.reshape(query_rows.shape), probability, prob_low)


def backprop(query_rows, key_rows, value_rows, probability, prob_low, upstream):
    factor = HEAD_DIM ** (-0.5)
    up_heads = heads_view(upstream)
    value_grad = jnp.einsum(
        "phfe,fphd->ephd", prob_low, up_heads, preferred_element_type=jnp.float32
    ).astype(jnp.bfloat16)
    prob_grad = jnp.einsum(
        "fphd,ephd->phfe", up_heads, heads_view(value_rows), preferred_element_type=jnp.float32
    )
    centre = jnp.sum(probability * prob_grad, axis=-1, keepdims=True)
    score_grad = (probability * (prob_grad - centre) * factor).astype(jnp.bfloat16)
    query_grad = jnp.einsum(
        "phfe,ephd->fphd", score_grad, heads_view(key_rows), preferred_element_type=jnp.float32
    ).astype(jnp.bfloat16)
    key_grad = jnp.einsum(
        "phfe,fphd->ephd", score_grad, heads_view(query_rows), preferred_element_type=jnp.float32
    ).astype(jnp.bfloat16)
    shaped = query_rows.shape
    return (query_grad.reshape(shaped), key_grad.reshape(shaped), value_grad.reshape(shaped))


def transposed_product(left_rows, right_rows):
    return lax.dot_general(
        left_rows, right_rows, (((0,), (0,)), ((), ())), preferred_element_type=jnp.float32
    )


def on_device(queries, keys, values, cotangent, out_weight):
    features = queries.shape[3]
    weight = lax.all_gather(out_weight, "fsdp", axis=0, tiled=True)
    query_patch, key_patch, value_patch = (
        lax.all_to_all(queries, "seq", split_axis=2, concat_axis=1, tiled=True),
        lax.all_to_all(keys, "seq", split_axis=2, concat_axis=1, tiled=True),
        lax.all_to_all(values, "seq", split_axis=2, concat_axis=1, tiled=True),
    )
    attended, probability, prob_low = attend(query_patch[0], key_patch[0], value_patch[0])
    att_frames = lax.all_to_all(attended[None], "seq", split_axis=1, concat_axis=2, tiled=True)
    att_rows = att_frames.reshape(-1, features)
    cot_rows = cotangent.reshape(-1, features)
    output = jnp.dot(att_rows, weight, preferred_element_type=jnp.float32).astype(jnp.bfloat16)
    output = output.reshape(queries.shape)
    up_frames = lax.dot_general(
        cot_rows, weight, (((1,), (1,)), ((), ())), preferred_element_type=jnp.float32
    ).astype(jnp.bfloat16)
    upstream = lax.all_to_all(
        up_frames.reshape(queries.shape), "seq", split_axis=2, concat_axis=1, tiled=True
    )[0]
    query_local, key_local, value_local = backprop(
        query_patch[0], key_patch[0], value_patch[0], probability, prob_low, upstream
    )
    query_grad, key_grad, value_grad = (
        lax.all_to_all(query_local[None], "seq", split_axis=1, concat_axis=2, tiled=True),
        lax.all_to_all(key_local[None], "seq", split_axis=1, concat_axis=2, tiled=True),
        lax.all_to_all(value_local[None], "seq", split_axis=1, concat_axis=2, tiled=True),
    )
    row_share = lax.psum_scatter(
        transposed_product(att_rows, cot_rows), "fsdp", scatter_dimension=0, tiled=True
    )
    weight_grad = lax.psum_scatter(row_share, "seq", scatter_dimension=1, tiled=True)
    return (output, query_grad, key_grad, value_grad, weight_grad)


def solution(mesh):
    placed = (
        P("fsdp", "seq", None, None),
        P("fsdp", "seq", None, None),
        P("fsdp", "seq", None, None),
        P("fsdp", "seq", None, None),
        P("fsdp", None),
    )
    return jax.shard_map(
        on_device,
        mesh=mesh,
        in_specs=placed,
        out_specs=(
            P("fsdp", "seq", None, None),
            P("fsdp", "seq", None, None),
            P("fsdp", "seq", None, None),
            P("fsdp", "seq", None, None),
            P("fsdp", "seq"),
        ),
        check_vma=False,
    )
```

profile of v0, /device:TPU:2, one launch (start us, length us, event | category | flops | bytes accessed | tf_op | source)
XLA Modules:
  0.0 1134.3 jit_solution(7269443782486266706)
XLA Ops:
  7.2 3.6 copy.78
  10.8 12.2 %all-to-all-start.2 = ((bf16[1,2,256,1152]{3,1,0,2:T(2,128)(2,1)}), bf16[1,2,256,1152]{3,1,0,2:T(2,128)(2,1)S(1)}, u32[]{:S(2)}, u32[]{:S(2)}) async-start(bf16[1,2,256,1152]{3,1,0,2:T(2,128)(2,1)} %copy.78), calls=%async_computation.2 | async-start | bytes 2359296 | tf_op jit(solution)/shard_map/all_to_all | solution.py:68
  23.0 2.2 copy.72
  25.2 28.9 %all-to-all-done.2 = bf16[1,2,256,1152]{3,1,0,2:T(2,128)(2,1)S(1)} async-done(((bf16[1,2,256,1152]{3,1,0,2:T(2,128)(2,1)}), bf16[1,2,256,1152]{3,1,0,2:T(2,128)(2,1)S(1)}, u32[]{:S(2)}, u32[]{:S(2)}) %all-to-all-start.2) | async-done | bytes 1179680 | tf_op jit(solution)/shard_map/all_to_all | solution.py:68
  54.1 6.0 all-to-all-start
  60.1 3.5 copy.74
  63.6 27.1 %all-to-all-done = bf16[1,2,256,1152]{3,1,0,2:T(2,128)(2,1)S(1)} async-done(((bf16[1,2,256,1152]{3,1,0,2:T(2,128)(2,1)}), bf16[1,2,256,1152]{3,1,0,2:T(2,128)(2,1)S(1)}, u32[]{:S(2)}, u32[]{:S(2)}) %all-to-all-start) | async-done | bytes 1179680 | tf_op jit(solution)/shard_map/all_to_all | solution.py:66
  90.7 6.3 all-to-all-start.1
  98.3 1.5 copy.113
  99.8 5.1 reshape_squeeze.17
  104.9 2.9 copy.81
  107.8 2.7 copy.115
  110.5 5.1 reshape_squeeze.15
  115.6 2.9 copy.76
  118.5 37.4 %all-to-all-done.1 = bf16[1,2,256,1152]{3,1,0,2:T(2,128)(2,1)} async-done(((bf16[1,2,256,1152]{3,1,0,2:T(2,128)(2,1)}), bf16[1,2,256,1152]{3,1,0,2:T(2,128)(2,1)}, u32[]{:S(2)}, u32[]{:S(2)}) %all-to-all-start.1) | async-done | bytes 1179680 | tf_op jit(solution)/shard_map/all_to_all | solution.py:67
  156.0 2.7 copy.114
  158.7 5.1 reshape_squeeze.16
  163.8 2.9 copy.77
  166.7 6.0 fusion.32
  172.7 3.0 convolution_convert_fusion.3
  176.6 36.6 %all_to_all.129 = bf16[1,128,4,1152]{3,2,0,1:T(4,128)(2,1)S(1)} all-to-all(bf16[1,128,4,1152]{3,2,0,1:T(4,128)(2,1)S(1)} %copy.82), channel_id=1, replica_groups=mesh['seq'=64,'fsdp'=4] {'seq'}, dimensions={1} | all-to-all | bytes 2359296 | tf_op jit(solution)/shard_map/all_to_all | solution.py:71
  213.2 1.4 copy.83
  214.6 2.4 reshape.30
  217.0 4.1 fusion.34
  221.1 3.6 convolution_convert_fusion
  224.7 1.2 copy.84
  226.0 93.4 %all_to_all.130 = bf16[1,2,256,1152]{3,1,0,2:T(2,128)(2,1)S(1)} all-to-all(bf16[1,2,256,1152]{3,1,0,2:T(2,128)(2,1)S(1)} %copy.84), channel_id=1, replica_groups=mesh['seq'=64,'fsdp'=4] {'seq'}, dimensions={2} | all-to-all | bytes 2359296 | tf_op jit(solution)/shard_map/all_to_all | solution.py:79
  319.3 1.5 copy.85
  320.8 5.1 reshape_squeeze.18
  325.9 2.9 copy.86
  328.8 4.6 fusion.33
  333.4 8.5 fusion.17
  341.9 3.4 copy.90
  345.3 6.8 all-to-all-start.5
  352.2 8.4 fusion.20
  360.6 3.4 copy.94
  364.0 18.4 %all-to-all-done.5 = bf16[1,128,4,1152]{3,2,0,1:T(4,128)(2,1)} async-done(((bf16[1,128,4,1152]{3,2,0,1:T(4,128)(2,1)}), bf16[1,128,4,1152]{3,2,0,1:T(4,128)(2,1)}, u32[]{:S(2)}, u32[]{:S(2)}) %all-to-all-start.5) | async-done | bytes 1179680 | tf_op jit(solution)/shard_map/all_to_all | solution.py:86
  382.4 6.3 all-to-all-start.6
  388.8 4.8 convolution_convert_fusion.2
  393.6 3.4 copy.98
  397.0 22.2 %all-to-all-done.6 = bf16[1,128,4,1152]{3,2,0,1:T(4,128)(2,1)} async-done(((bf16[1,128,4,1152]{3,2,0,1:T(4,128)(2,1)}), bf16[1,128,4,1152]{3,2,0,1:T(4,128)(2,1)}, u32[]{:S(2)}, u32[]{:S(2)}) %all-to-all-start.6) | async-done | bytes 1179680 | tf_op jit(solution)/shard_map/all_to_all | solution.py:87
  419.2 6.0 all-to-all-start.7
  427.2 4.6 convolution_convert_fusion.1
  431.8 2.2 copy.91
  434.0 1.1 copy.100
  435.1 2.2 copy.95
  438.5 17.7 %all-to-all-done.7 = bf16[1,128,4,1152]{3,2,0,1:T(4,128)(2,1)S(1)} async-done(((bf16[1,128,4,1152]{3,2,0,1:T(4,128)(2,1)}), bf16[1,128,4,1152]{3,2,0,1:T(4,128)(2,1)S(1)}, u32[]{:S(2)}, u32[]{:S(2)}) %all-to-all-start.7) | async-done | bytes 1179680 | tf_op jit(solution)/shard_map/all_to_all | solution.py:88
  458.3 667.5 %all-reduce.3.cloned.1.call-done = f32[288,1152]{1,0:T(8,128)} async-done(((f32[288,1152]{1,0:T(8,128)}), f32[288,1152]{1,0:T(8,128)}) %all-reduce.3.cloned.1.call-update) | async-done | bytes 1327120
  (35 shorter events, 8.5 us)
Async XLA Ops:
  7.2 209.8 %copy-start = (bf16[1,2,256,1152]{3,2,1,0:T(8,128)(2,1)S(1)}, bf16[1,2,256,1152]{3,2,1,0:T(8,128)(2,1)}, u32[]{:S(2)}) copy-start(bf16[1,2,256,1152]{3,2,1,0:T(8,128)(2,1)} %param.8) | copy-start | bytes 3538948
  10.8 12.2 %copy-start.7 = (bf16[1,2,256,1152]{3,2,1,0:T(8,128)(2,1)S(1)}, bf16[1,2,256,1152]{3,2,1,0:T(8,128)(2,1)}, u32[]{:S(2)}) copy-start(bf16[1,2,256,1152]{3,2,1,0:T(8,128)(2,1)} %param.5) | copy-start | bytes 3538948
  10.8 43.3 %all-to-all-start.2 = ((bf16[1,2,256,1152]{3,1,0,2:T(2,128)(2,1)}), bf16[1,2,256,1152]{3,1,0,2:T(2,128)(2,1)S(1)}, u32[]{:S(2)}, u32[]{:S(2)}) async-start(bf16[1,2,256,1152]{3,1,0,2:T(2,128)(2,1)} %copy.78), calls=%async_computation.2 | async-start | bytes 2359296 | tf_op jit(solution)/shard_map/all_to_all | solution.py:68
  54.1 36.6 %all-to-all-start = ((bf16[1,2,256,1152]{3,1,0,2:T(2,128)(2,1)}), bf16[1,2,256,1152]{3,1,0,2:T(2,128)(2,1)S(1)}, u32[]{:S(2)}, u32[]{:S(2)}) async-start(bf16[1,2,256,1152]{3,1,0,2:T(2,128)(2,1)} %copy.72), calls=%async_computation | async-start | bytes 2359296 | tf_op jit(solution)/shard_map/all_to_all | solution.py:66
  90.7 7.1 copy-start.4
  90.7 65.2 %all-to-all-start.1 = ((bf16[1,2,256,1152]{3,1,0,2:T(2,128)(2,1)}), bf16[1,2,256,1152]{3,1,0,2:T(2,128)(2,1)}, u32[]{:S(2)}, u32[]{:S(2)}) async-start(bf16[1,2,256,1152]{3,1,0,2:T(2,128)(2,1)} %copy.74), calls=%async_computation.1 | async-start | bytes 2359296 | tf_op jit(solution)/shard_map/all_to_all | solution.py:67
  97.1 124.0 %all-gather.2.cloned.1.call-start = ((), (), s32[]{:S(2)}) async-start(), calls=%async_computation.9 | async-start | bytes 3317760 | tf_op jit(solution)/shard_map/all_gather | solution.py:64
  97.8 327.5 %reduce-scatter.3.cloned.1.call-start = ((), (), s32[]{:S(2)}) async-start(), calls=%async_computation.10 | async-start | bytes 6635520 | tf_op jit(solution)/shard_map/reduce_scatter | solution.py:90
  166.7 6.0 copy-start.2
  328.8 4.6 copy-start.6
  328.8 4.6 copy-start.9
  345.3 6.9 copy-start.5
  345.3 37.1 %all-to-all-start.5 = ((bf16[1,128,4,1152]{3,2,0,1:T(4,128)(2,1)}), bf16[1,128,4,1152]{3,2,0,1:T(4,128)(2,1)}, u32[]{:S(2)}, u32[]{:S(2)}) async-start(bf16[1,128,4,1152]{3,2,0,1:T(4,128)(2,1)} %copy.90), calls=%async_computation.5 | async-start | bytes 2359296 | tf_op jit(solution)/shard_map/all_to_all | solution.py:86
  364.0 24.8 %copy-start.3 = (bf16[128,4,16,72]{0,3,2,1:T(8,128)(2,1)S(1)}, bf16[128,4,16,72]{0,3,2,1:T(8,128)(2,1)}, u32[]{:S(2)}) copy-start(bf16[128,4,16,72]{0,3,2,1:T(8,128)(2,1)} %copy.86) | copy-start | bytes 3538948
  382.4 36.8 %all-to-all-start.6 = ((bf16[1,128,4,1152]{3,2,0,1:T(4,128)(2,1)}), bf16[1,128,4,1152]{3,2,0,1:T(4,128)(2,1)}, u32[]{:S(2)}, u32[]{:S(2)}) async-start(bf16[1,128,4,1152]{3,2,0,1:T(4,128)(2,1)} %copy.94), calls=%async_computation.6 | async-start | bytes 2359296 | tf_op jit(solution)/shard_map/all_to_all | solution.py:87
  419.2 37.0 %all-to-all-start.7 = ((bf16[1,128,4,1152]{3,2,0,1:T(4,128)(2,1)}), bf16[1,128,4,1152]{3,2,0,1:T(4,128)(2,1)S(1)}, u32[]{:S(2)}, u32[]{:S(2)}) async-start(bf16[1,128,4,1152]{3,2,0,1:T(4,128)(2,1)} %copy.98), calls=%async_computation.7 | async-start | bytes 2359296 | tf_op jit(solution)/shard_map/all_to_all | solution.py:88
  425.2 0.8 copy-start.8
  425.2 700.5 %all-reduce.3.cloned.1.call-start = ((), (), s32[]{:S(2)}) async-start(), calls=%async_computation.11 | async-start | bytes 2654208
  457.1 670.4 %copy-start.1 = (bf16[1,2,256,1152]{3,2,1,0:T(8,128)(2,1)S(1)}, bf16[1,2,256,1152]{3,2,1,0:T(8,128)(2,1)}, u32[]{:S(2)}) copy-start(bf16[1,2,256,1152]{3,2,1,0:T(8,128)(2,1)} %param.8) | copy-start | bytes 3538948
Sparse Core Ops, SparseCore 0:
  99.7 41.2 all-gather.1
  221.2 72.4 reduce-scatter.2
  428.9 696.8 all-reduce.2
where the time goes:
time: 1140 us; the launch traced here: 1130 us
  waiting for transfers between devices  821 us (72%)
  blocking collectives  130 us (11%)
  local copies, waits for them, and re-layouts  77 us (7%)
  matrix products  47.6 us (4%)
  starting transfers between devices  44.3 us (4%)
  between operations  14.9 us (1%)
    unnamed x4, waiting for transfers between devices  669 us
    all_to_all x1, blocking collectives, on_device(): lax.all_to_all(up_frames.reshape(queries.shape), 'seq', split_axis=2, con...  93.4 us
    all_to_all x1, waiting for transfers between devices, on_device(): lax.all_to_all(keys, 'seq', split_axis=2, concat_axis=1, tiled=True)  37.4 us
    all_to_all x1, blocking collectives, on_device(): lax.all_to_all(attended[None], 'seq', split_axis=1, concat_axis=2, tiled=...  36.6 us
    another operation x8, local copies, waits for them, and re-layouts, heads_view(): return tensor.reshape(tensor.shape[0], tensor.shape[1], HEADS, HEAD_DIM)  31.9 us
    all_to_all x1, waiting for transfers between devices, on_device(): lax.all_to_all(values, 'seq', split_axis=2, concat_axis=1, tiled=True)  28.9 us
    all_to_all x1, waiting for transfers between devices, on_device(): lax.all_to_all(queries, 'seq', split_axis=2, concat_axis=1, tiled=True)  27.1 us
  transfers between devices with their start and end apart: 9, of which 7 were waited for; matrix products, arithmetic and copies ran while one was open for 11% of the time, Pallas kernels for 0%

commit v1 on v0

--- a/solution.py
+++ b/solution.py
@@ -84,7 +84,12 @@
     )
     query_grad, key_grad, value_grad = (
         lax.all_to_all(query_local[None], "seq", split_axis=1, concat_axis=2, tiled=True),
-        lax.all_to_all(key_local[None], "seq", split_axis=1, concat_axis=2, tiled=True),
+        jnp.concatenate(
+            lax.all_to_all(
+                jnp.stack(jnp.split(key_local[None], lax.axis_size("seq"), axis=1)), "seq", 0, 0
+            ),
+            axis=2,
+        ),
         lax.all_to_all(value_local[None], "seq", split_axis=1, concat_axis=2, tiled=True),
     )
     row_share = lax.psum_scatter(

time: 1140 us -> 1210 us (1.061)
  local copies, waits for them, and re-layouts: 77 us -> 235 us
  blocking collectives: 130 us -> 0 us
  waiting for transfers between devices: 821 us -> 848 us
  starting transfers between devices: 44.3 us -> 61.4 us
    all_to_all x2 -> x0, blocking collectives: 130 us -> none  [the longest x1 93.4 us: on_device(): lax.all_to_all(up_frames.reshape(queries.shape), 'seq', split_axis=2, con...]
    unnamed x29 -> x200, local copies, waits for them, and re-layouts: 15.2 us -> 136 us
    all_to_all x1 -> x3, waiting for transfers between devices: 22.2 us -> 64.7 us  [the longest x1 24.8 us: on_device(): lax.all_to_all(attended[None], 'seq', split_axis=1, concat_axis=2, tiled=...]
    split x0 -> x4, local copies, waits for them, and re-layouts: none -> 36.5 us  [on_device(): jnp.split(key_local[None], lax.axis_size('seq'), axis=1)]
    all_to_all x1, waiting for transfers between devices: 17.7 us -> 0.01 us  [on_device(): lax.all_to_all(value_local[None], 'seq', split_axis=1, concat_axis=2, til...]
  transfers between devices with their start and end apart: 9 -> 11, of which waited for: 7 -> 8; matrix products, arithmetic and copies ran while one was open for 11% -> 23% of each run, Pallas kernels for 0% -> 0%
where the time goes in v1:
time: 1210 us; the launch traced here: 1200 us
  waiting for transfers between devices  848 us (70%)
  local copies, waits for them, and re-layouts  235 us (19%)
  starting transfers between devices  61.4 us (5%)
  matrix products  44.8 us (4%)
  between operations  15 us (1%)
    unnamed x4, waiting for transfers between devices  669 us
    unnamed x200, local copies, waits for them, and re-layouts  136 us
    all_to_all x1, waiting for transfers between devices, on_device(): lax.all_to_all(values, 'seq', split_axis=2, concat_axis=1, tiled=True)  38 us
    split x4, local copies, waits for them, and re-layouts, on_device(): jnp.split(key_local[None], lax.axis_size('seq'), axis=1)  36.5 us
    another operation x8, local copies, waits for them, and re-layouts, heads_view(): return tensor.reshape(tensor.shape[0], tensor.shape[1], HEADS, HEAD_DIM)  31.9 us
    all_to_all x1, waiting for transfers between devices, on_device(): lax.all_to_all(queries, 'seq', split_axis=2, concat_axis=1, tiled=True)  28.9 us
    all_to_all x1, waiting for transfers between devices, on_device(): lax.all_to_all(keys, 'seq', split_axis=2, concat_axis=1, tiled=True)  27.1 us
    all_to_all x1, waiting for transfers between devices, on_device(): lax.all_to_all(attended[None], 'seq', split_axis=1, concat_axis=2, tiled=...  24.8 us
  transfers between devices with their start and end apart: 11, of which 8 were waited for; matrix products, arithmetic and copies ran while one was open for 23% of the time, Pallas kernels for 0%

profile of v1, /device:TPU:2, one launch (start us, length us, event | category | flops | bytes accessed | tf_op | source)
XLA Modules:
  0.0 1204.1 jit_solution(7831674596159615746)
XLA Ops:
  7.2 3.6 copy.324
  10.8 12.2 %all-to-all-start = ((bf16[1,2,256,1152]{3,1,0,2:T(2,128)(2,1)}), bf16[1,2,256,1152]{3,1,0,2:T(2,128)(2,1)S(1)}, u32[]{:S(2)}, u32[]{:S(2)}) async-start(bf16[1,2,256,1152]{3,1,0,2:T(2,128)(2,1)} %copy.324), calls=%async_computation | async-start | bytes 2359296 | tf_op jit(solution)/shard_map/all_to_all | solution.py:66
  23.0 2.2 copy.326
  25.2 28.9 %all-to-all-done = bf16[1,2,256,1152]{3,1,0,2:T(2,128)(2,1)S(1)} async-done(((bf16[1,2,256,1152]{3,1,0,2:T(2,128)(2,1)}), bf16[1,2,256,1152]{3,1,0,2:T(2,128)(2,1)S(1)}, u32[]{:S(2)}, u32[]{:S(2)}) %all-to-all-start) | async-done | bytes 1179680 | tf_op jit(solution)/shard_map/all_to_all | solution.py:66
  54.1 6.0 all-to-all-start.1
  60.1 3.5 copy.330
  63.6 27.1 %all-to-all-done.1 = bf16[1,2,256,1152]{3,1,0,2:T(2,128)(2,1)S(1)} async-done(((bf16[1,2,256,1152]{3,1,0,2:T(2,128)(2,1)}), bf16[1,2,256,1152]{3,1,0,2:T(2,128)(2,1)S(1)}, u32[]{:S(2)}, u32[]{:S(2)}) %all-to-all-start.1) | async-done | bytes 1179680 | tf_op jit(solution)/shard_map/all_to_all | solution.py:67
  90.7 6.3 all-to-all-start.2
  99.3 5.1 reshape_squeeze.15
  104.4 2.9 copy.328
  107.3 2.7 copy.493
  110.0 5.1 reshape_squeeze.16
  115.1 2.9 copy.329
  118.0 38.0 %all-to-all-done.2 = bf16[1,2,256,1152]{3,1,0,2:T(2,128)(2,1)} async-done(((bf16[1,2,256,1152]{3,1,0,2:T(2,128)(2,1)}), bf16[1,2,256,1152]{3,1,0,2:T(2,128)(2,1)}, u32[]{:S(2)}, u32[]{:S(2)}) %all-to-all-start.2) | async-done | bytes 1179680 | tf_op jit(solution)/shard_map/all_to_all | solution.py:68
  156.0 2.7 copy.492
  158.7 5.1 reshape_squeeze.17
  163.8 2.9 copy.333
  166.7 6.0 fusion.36
  172.7 3.0 convolution_convert_fusion.3
  177.7 6.0 all-to-all-start.3
  183.7 3.6 convolution_convert_fusion
  187.3 2.2 copy.336
  189.6 24.8 %all-to-all-done.3 = bf16[1,128,4,1152]{3,2,0,1:T(4,128)(2,1)S(1)} async-done(((bf16[1,128,4,1152]{3,2,0,1:T(4,128)(2,1)}), bf16[1,128,4,1152]{3,2,0,1:T(4,128)(2,1)S(1)}, u32[]{:S(2)}, u32[]{:S(2)}) %all-to-all-start.3) | async-done | bytes 1179680 | tf_op jit(solution)/shard_map/all_to_all | solution.py:71
  214.3 6.3 all-to-all-start.4
  222.3 2.4 reshape.36
  224.7 4.1 fusion.38
  228.8 22.3 %all-to-all-done.4 = bf16[1,2,256,1152]{3,1,0,2:T(2,128)(2,1)} async-done(((bf16[1,2,256,1152]{3,1,0,2:T(2,128)(2,1)}), bf16[1,2,256,1152]{3,1,0,2:T(2,128)(2,1)}, u32[]{:S(2)}, u32[]{:S(2)}) %all-to-all-start.4) | async-done | bytes 1179680 | tf_op jit(solution)/shard_map/all_to_all | solution.py:79
  251.1 2.7 copy.337
  253.9 5.1 reshape_squeeze.18
  258.9 2.9 copy.338
  261.9 4.6 fusion.37
  266.5 2.6 convolution_convert_fusion.2
  269.1 7.8 fusion.20
  276.9 4.3 fusion.35
  281.2 10.6 fusion.33
  291.8 10.8 fusion.34
  302.6 10.7 fusion.32
  313.4 3.4 copy.413
  316.8 6.7 all-to-all-start.7
  424.8 8.5 fusion.17
  433.3 3.4 copy.342
  447.6 10.9 all-to-all-start.5
  468.2 20.3 %all-to-all-done.5 = bf16[1,128,4,1152]{3,2,0,1:T(4,128)(2,1)} async-done(((bf16[1,128,4,1152]{3,2,0,1:T(4,128)(2,1)}), bf16[1,128,4,1152]{3,2,0,1:T(4,128)(2,1)}, u32[]{:S(2)}, u32[]{:S(2)}) %all-to-all-start.5) | async-done | bytes 1179680 | tf_op jit(solution)/shard_map/all_to_all | solution.py:86
  488.5 6.0 all-to-all-start.6
  496.5 4.6 convolution_convert_fusion.1
  501.1 2.2 copy.414
  507.8 17.6 %all-to-all-done.6 = bf16[64,1,2,4,1152]{4,3,2,1,0:T(4,128)(2,1)S(1)} async-done(((bf16[64,1,2,4,1152]{4,3,2,1,0:T(4,128)(2,1)}), bf16[64,1,2,4,1152]{4,3,2,1,0:T(4,128)(2,1)S(1)}, u32[]{:S(2)}, u32[]{:S(2)}) %all-to-all-start.6) | async-done | bytes 1179680 | tf_op jit(solution)/shard_map/all_to_all | solution.py:88
  527.4 668.1 %all-reduce.3.cloned.1.call-done = f32[288,1152]{1,0:T(8,128)} async-done(((f32[288,1152]{1,0:T(8,128)}), f32[288,1152]{1,0:T(8,128)}) %all-reduce.3.cloned.1.call-update) | async-done | bytes 1327120
  (212 shorter events, 137.2 us)
Async XLA Ops:
  7.2 176.5 %copy-start = (bf16[1,2,256,1152]{3,2,1,0:T(8,128)(2,1)S(1)}, bf16[1,2,256,1152]{3,2,1,0:T(8,128)(2,1)}, u32[]{:S(2)}) copy-start(bf16[1,2,256,1152]{3,2,1,0:T(8,128)(2,1)} %param.8) | copy-start | bytes 3538948
  10.8 12.2 %copy-start.28 = (bf16[1,2,256,1152]{3,2,1,0:T(8,128)(2,1)S(1)}, bf16[1,2,256,1152]{3,2,1,0:T(8,128)(2,1)}, u32[]{:S(2)}) copy-start(bf16[1,2,256,1152]{3,2,1,0:T(8,128)(2,1)} %param.6) | copy-start | bytes 3538948
  10.8 43.3 %all-to-all-start = ((bf16[1,2,256,1152]{3,1,0,2:T(2,128)(2,1)}), bf16[1,2,256,1152]{3,1,0,2:T(2,128)(2,1)S(1)}, u32[]{:S(2)}, u32[]{:S(2)}) async-start(bf16[1,2,256,1152]{3,1,0,2:T(2,128)(2,1)} %copy.324), calls=%async_computation | async-start | bytes 2359296 | tf_op jit(solution)/shard_map/all_to_all | solution.py:66
  54.1 36.6 %all-to-all-start.1 = ((bf16[1,2,256,1152]{3,1,0,2:T(2,128)(2,1)}), bf16[1,2,256,1152]{3,1,0,2:T(2,128)(2,1)S(1)}, u32[]{:S(2)}, u32[]{:S(2)}) async-start(bf16[1,2,256,1152]{3,1,0,2:T(2,128)(2,1)} %copy.326), calls=%async_computation.1 | async-start | bytes 2359296 | tf_op jit(solution)/shard_map/all_to_all | solution.py:67
  90.7 7.1 copy-start.26
  90.7 65.2 %all-to-all-start.2 = ((bf16[1,2,256,1152]{3,1,0,2:T(2,128)(2,1)}), bf16[1,2,256,1152]{3,1,0,2:T(2,128)(2,1)}, u32[]{:S(2)}, u32[]{:S(2)}) async-start(bf16[1,2,256,1152]{3,1,0,2:T(2,128)(2,1)} %copy.330), calls=%async_computation.2 | async-start | bytes 2359296 | tf_op jit(solution)/shard_map/all_to_all | solution.py:68
  97.1 86.6 %all-gather.2.cloned.1.call-start = ((), (), s32[]{:S(2)}) async-start(), calls=%async_computation.9 | async-start | bytes 3317760 | tf_op jit(solution)/shard_map/all_gather | solution.py:64
  166.7 6.0 copy-start.24
  177.7 36.7 %all-to-all-start.3 = ((bf16[1,128,4,1152]{3,2,0,1:T(4,128)(2,1)}), bf16[1,128,4,1152]{3,2,0,1:T(4,128)(2,1)S(1)}, u32[]{:S(2)}, u32[]{:S(2)}) async-start(bf16[1,128,4,1152]{3,2,0,1:T(4,128)(2,1)} %copy.334), calls=%async_computation.3 | async-start | bytes 2359296 | tf_op jit(solution)/shard_map/all_to_all | solution.py:71
  214.3 36.8 %all-to-all-start.4 = ((bf16[1,2,256,1152]{3,1,0,2:T(2,128)(2,1)}), bf16[1,2,256,1152]{3,1,0,2:T(2,128)(2,1)}, u32[]{:S(2)}, u32[]{:S(2)}) async-start(bf16[1,2,256,1152]{3,1,0,2:T(2,128)(2,1)} %copy.336), calls=%async_computation.4 | async-start | bytes 2359296 | tf_op jit(solution)/shard_map/all_to_all | solution.py:79
  220.7 274.1 %reduce-scatter.3.cloned.1.call-start = ((), (), s32[]{:S(2)}) async-start(), calls=%async_computation.10 | async-start | bytes 6635520 | tf_op jit(solution)/shard_map/reduce_scatter | solution.py:95
  261.9 4.6 copy-start.25
  261.9 4.6 copy-start.30
  261.9 4.6 copy-start.31
  316.8 130.8 %all-to-all-start.7 = ((bf16[1,128,4,1152]{3,2,0,1:T(4,128)(2,1)}), bf16[1,128,4,1152]{3,2,0,1:T(4,128)(2,1)}, u32[]{:S(2)}, u32[]{:S(2)}) async-start(bf16[1,128,4,1152]{3,2,0,1:T(4,128)(2,1)} %copy.413), calls=%async_computation.7 | async-start | bytes 2359296 | tf_op jit(solution)/shard_map/all_to_all | solution.py:93
  323.5 1.8 copy-start.23
  325.8 3.5 copy-start.22
  329.7 4.1 copy-start.21
  334.3 3.5 copy-start.20
  338.2 3.5 copy-start.19
  342.1 3.5 copy-start.18
  346.0 3.5 copy-start.17
  349.9 3.5 copy-start.16
  353.8 3.5 copy-start.15
  357.8 3.5 copy-start.14
  361.7 3.5 copy-start.13
  365.6 3.5 copy-start.12
  369.5 3.5 copy-start.11
  373.4 3.6 copy-start.10
  377.5 3.5 copy-start.9
  381.4 3.5 copy-start.8
  385.3 3.5 copy-start.7
  389.3 3.5 copy-start.6
  393.2 31.6 %copy-start.27 = (bf16[128,4,16,72]{0,3,2,1:T(8,128)(2,1)S(1)}, bf16[128,4,16,72]{0,3,2,1:T(8,128)(2,1)}, u32[]{:S(2)}) copy-start(bf16[128,4,16,72]{0,3,2,1:T(8,128)(2,1)} %copy.329) | copy-start | bytes 3538948
  436.7 3.5 copy-start.5
  440.6 3.5 copy-start.4
  447.6 40.9 %all-to-all-start.5 = ((bf16[1,128,4,1152]{3,2,0,1:T(4,128)(2,1)}), bf16[1,128,4,1152]{3,2,0,1:T(4,128)(2,1)}, u32[]{:S(2)}, u32[]{:S(2)}) async-start(bf16[1,128,4,1152]{3,2,0,1:T(4,128)(2,1)} %copy.342), calls=%async_computation.5 | async-start | bytes 2359296 | tf_op jit(solution)/shard_map/all_to_all | solution.py:86
  458.5 2.3 copy-start.3
  461.2 3.5 copy-start.2
  488.5 36.8 %all-to-all-start.6 = ((bf16[64,1,2,4,1152]{4,3,2,1,0:T(4,128)(2,1)}), bf16[64,1,2,4,1152]{4,3,2,1,0:T(4,128)(2,1)S(1)}, u32[]{:S(2)}, u32[]{:S(2)}) async-start(bf16[64,1,2,4,1152]{4,3,2,1,0:T(4,128)(2,1)} %constant_dynamic-update-slice_fusion), calls=%async_computation.6 | async-start | bytes 2359296 | tf_op jit(solution)/shard_map/all_to_all | solution.py:88
  494.5 0.8 copy-start.29
  494.5 701.0 %all-reduce.3.cloned.1.call-start = ((), (), s32[]{:S(2)}) async-start(), calls=%async_computation.11 | async-start | bytes 2654208
  526.2 671.1 %copy-start.1 = (bf16[1,2,256,1152]{3,2,1,0:T(8,128)(2,1)S(1)}, bf16[1,2,256,1152]{3,2,1,0:T(8,128)(2,1)}, u32[]{:S(2)}) copy-start(bf16[1,2,256,1152]{3,2,1,0:T(8,128)(2,1)} %param.8) | copy-start | bytes 3538948
Sparse Core Ops, SparseCore 0:
  99.7 41.2 all-gather.1
  228.9 95.7 reduce-scatter.2
  498.1 697.3 all-reduce.2
